TPU v7x, 32 devices: a whole 2x2x4 slice. The times are simulated.
32 devices in a mesh: expert: 4 (over x, core), shard: 8 (over z, y).
Axes of the slice: x: 2, y: 2, z: 4, core: 2. Of those that a mesh axis runs over, the one named last changes fastest.
Arguments:
- tokens: bfloat16 [8, 1024, 768], P('shard', 'expert'), may hold values from -22 to 22
- w_query: bfloat16 [768, 768], P('shard'), may hold values from -0.21875 to 0.21875
- w_key: bfloat16 [768, 768], P('shard'), may hold values from -0.21875 to 0.21875
- w_value: bfloat16 [768, 768], P('shard'), may hold values from -0.21875 to 0.21875
- w_output: bfloat16 [768, 768], P('shard'), may hold values from -2.5 to 2.5
- w_router: bfloat16 [768, 4], P('shard'), may hold values from -0.15625 to 0.15625
- norm_one: bfloat16 [768], P('shard'), may hold values from 0.5 to 1.5
- norm_two: bfloat16 [768], P('shard'), may hold values from 0.5 to 1.5
- rel_bias: bfloat16 [32, 12], P('shard'), may hold values from -4 to 4
- w_in: bfloat16 [4, 768, 3072], P('expert'), may hold values from -0.21875 to 0.21875
- w_out: bfloat16 [4, 3072, 768], P('expert'), may hold values from -1.25 to 1.25
- routes: int32 [8, 1024, 1], P('shard', 'expert'), may hold values from 0 to 3; in each aligned block of 256 rows (0 to 255, 256 to 511, ..., all dimensions but the last counted through in order) at most 128 rows name the same one
- seq_ids: int32 [8, 1024], P('shard'), may hold values from 0 to 2, as said below
- buckets: int32 [2047], replicated, may hold values from 0 to 31
- d_out: bfloat16 [8, 1024, 768], P('shard', 'expert'), may hold values from -6 to 6
Outputs:
- layer_out: bfloat16 [8, 1024, 768], P('shard', 'expert')
- d_tokens: float32 [8, 1024, 768], P('shard', 'expert')
- d_w_query: float32 [768, 768], P('shard')
- d_w_key: float32 [768, 768], P('shard')
- d_w_value: float32 [768, 768], P('shard')
- d_w_output: float32 [768, 768], P('shard')
- d_w_router: float32 [768, 4], P('shard')
- d_norm_one: float32 [768], P('shard')
- d_norm_two: float32 [768], P('shard')
- d_rel_bias: float32 [32, 12], P('shard')
- d_w_in: float32 [4, 768, 3072], P('expert', 'shard')
- d_w_out: float32 [4, 3072, 768], P('expert', 'shard')
Inputs may be any that keep to these rules, and one draw needn't show every extreme that they name: `routes`: among the rows of one device no expert is named more than 128 times, and in some device's rows one expert is named exactly 128 times. `seq_ids`: ids never fall along a sequence, and every sequence holds ids 0, 1 and 2.
All inputs are finite; a program needn't handle non-finite values.
Results may differ from a plain program's by a relative error of at most 0.04.
Values may be sent and summed in bfloat16 or wider, within the bound.
A program may use at most 192 MiB of HBM per device.

v0:
```python
import jax
import jax.numpy as jnp
from jax import lax
from jax.sharding import PartitionSpec as P

H = 12
HD = 64


EPSILON = 1e-06
NEGATIVE = -1e30
HIGHEST = lax.Precision.HIGHEST


def product(left, right):
    return jnp.dot(left, right, preferred_element_type=jnp.float32)


def norm_forward(values_in, gain):
    inverse = lax.rsqrt(jnp.mean(values_in * values_in, axis=-1, keepdims=True) + EPSILON)
    return (values_in * inverse * gain, inverse)


def norm_backward(values_in, inverse, gain, grad_in):
    scaled = grad_in * gain
    inner_mean = jnp.mean(scaled * values_in, axis=-1, keepdims=True)
    grad_out = inverse * scaled - values_in * (inverse * inverse * inverse) * inner_mean
    gain_grad = jnp.sum(grad_in * values_in * inverse, axis=0)
    return (grad_out, gain_grad)


def skew_bias(offset_bias, row_start, col_start, row_count, col_count, length):
    span_width = row_count + col_count - 1
    first_index = col_start - row_start + (length - row_count)
    window = lax.dynamic_slice_in_dim(offset_bias, first_index, span_width, 1)
    padded = jnp.pad(window, ((0, 0), (0, 1)))
    tiled_rows = jnp.tile(padded, (1, row_count))
    skewed = tiled_rows[:, : row_count * span_width].reshape(
        offset_bias.shape[0], row_count, span_width
    )
    return skewed[:, :, row_count - 1 :]


def raw_scores(query_heads, key_block):
    key_heads = key_block.reshape(key_block.shape[0], H, HD)
    return jnp.einsum("qhd,khd->hqk", query_heads, key_heads, preferred_element_type=jnp.float32)


def per_device(
    tokens,
    w_query,
    w_key,
    w_value,
    w_output,
    w_router,
    norm_one,
    norm_two,
    rel_bias,
    w_in,
    w_out,
    routes,
    seq_ids,
    buckets,
    d_out,
):
    row_count = tokens.shape[1]
    width = tokens.shape[2]
    flat_rows = tokens[0].astype(jnp.float32)
    query_all, key_all, value_all, output_all, router_all, gain_one, gain_two, table_low = (
        lax.all_gather(w_query, "shard", axis=0, tiled=True),
        lax.all_gather(w_key, "shard", axis=0, tiled=True),
        lax.all_gather(w_value, "shard", axis=0, tiled=True),
        lax.all_gather(w_output, "shard", axis=0, tiled=True),
        lax.all_gather(w_router, "shard", axis=0, tiled=True),
        lax.all_gather(norm_one, "shard", axis=0, tiled=True),
        lax.all_gather(norm_two, "shard", axis=0, tiled=True),
        lax.all_gather(rel_bias, "shard", axis=0, tiled=True),
    )
    gain_one_f = gain_one.astype(jnp.float32)
    gain_two_f = gain_two.astype(jnp.float32)
    bias_table = table_low.astype(jnp.float32)
    experts = router_all.shape[1]
    length = row_count * lax.axis_size("expert")
    row_start = lax.axis_index("expert") * row_count
    ids_all = seq_ids[0]
    ids_rows = lax.dynamic_slice_in_dim(ids_all, row_start, row_count)
    score_scale = HD ** (-0.5)
    h_one, inverse_one = norm_forward(flat_rows, gain_one_f)
    h_one_low = h_one.astype(jnp.bfloat16)
    query_low = product(h_one_low, query_all).astype(jnp.bfloat16)
    key_low = product(h_one_low, key_all).astype(jnp.bfloat16)
    value_low = product(h_one_low, value_all).astype(jnp.bfloat16)
    keys_full, values_full = (
        lax.all_gather(key_low, "expert", axis=0, tiled=True),
        lax.all_gather(value_low, "expert", axis=0, tiled=True),
    )
    bucket_hot = (
        buckets[:, None] == jnp.arange(bias_table.shape[0], dtype=jnp.int32)[None, :]
    ).astype(jnp.float32)
    offset_bias = jnp.einsum("ob,bh->ho", bucket_hot, bias_table, precision=HIGHEST)
    block_count = max(1, length // 512)
    key_rows = length // block_count
    ids_blocks = ids_all.reshape(block_count, key_rows)
    query_heads = query_low.reshape(row_count, H, HD)
    bias_rows, bias_back = jax.vjp(
        lambda table_rows: skew_bias(table_rows, row_start, 0, row_count, length, length),
        offset_bias,
    )
    bias_blocks = jnp.transpose(
        bias_rows.reshape(H, row_count, block_count, key_rows), (2, 0, 1, 3)
    )

    def masked_scores(key_block, ids_block, score_bias):
        same_doc = ids_rows[:, None] == ids_block[None, :]
        return jnp.where(
            same_doc[None], raw_scores(query_heads, key_block) * score_scale + score_bias, NEGATIVE
        )

    def first_pass(state, item):
        row_peak, row_total = state
        key_block, ids_block, score_bias = item
        scores = masked_scores(key_block, ids_block, score_bias)
        new_peak = jnp.maximum(row_peak, jnp.max(scores, axis=-1))
        row_total = row_total * jnp.exp(row_peak - new_peak) + jnp.sum(
            jnp.exp(scores - new_peak[..., None]), axis=-1
        )
        return ((new_peak, row_total), scores)

    start_state = (
        jnp.full((H, row_count), NEGATIVE, jnp.float32),
        jnp.zeros((H, row_count), jnp.float32),
    )
    key_blocks = keys_full.reshape(block_count, key_rows, width)
    value_blocks = values_full.reshape(block_count, key_rows, width)
    (row_peak, row_total), kept_scores = lax.scan(
        first_pass, start_state, (key_blocks, ids_blocks, bias_blocks)
    )
    log_total = row_peak + jnp.log(row_total)

    def second_pass(running, item):
        scores, value_block = item
        weights = jnp.exp(scores - log_total[..., None]).astype(jnp.bfloat16)
        value_heads = value_block.reshape(key_rows, H, HD)
        return (
            running
            + jnp.einsum("hqk,khd->qhd", weights, value_heads, preferred_element_type=jnp.float32),
            None,
        )

    mixed, _ = lax.scan(
        second_pass, jnp.zeros((row_count, H, HD), jnp.float32), (kept_scores, value_blocks)
    )
    mixed_rows = mixed.reshape(row_count, width)
    attn_low = mixed_rows.astype(jnp.bfloat16)
    x_one = flat_rows + product(attn_low, output_all)
    h_two, inverse_two = norm_forward(x_one, gain_two_f)
    h_two_low = h_two.astype(jnp.bfloat16)
    router_probs = jax.nn.softmax(product(h_two_low, router_all), axis=-1)
    route_ids = routes[0, :, 0]
    chosen_int = (route_ids[:, None] == jnp.arange(experts, dtype=jnp.int32)[None, :]).astype(
        jnp.int32
    )
    chosen = chosen_int.astype(jnp.float32)
    gate_value = jnp.sum(router_probs * chosen, axis=1)
    capacity = 2 * row_count // experts
    rank_index = jnp.sum((jnp.cumsum(chosen_int, axis=0) - chosen_int) * chosen_int, axis=1)
    slot_index = route_ids * capacity + rank_index
    placement = (
        jnp.arange(experts * capacity, dtype=jnp.int32)[:, None] == slot_index[None, :]
    ).astype(jnp.bfloat16)
    send_rows = product(placement, h_two_low).astype(jnp.bfloat16).reshape(experts, capacity, width)
    received = lax.all_to_all(send_rows, "expert", split_axis=0, concat_axis=0, tiled=True).reshape(
        experts * capacity, width
    )
    pre_act = product(received, w_in[0])
    act_low = jax.nn.gelu(pre_act, approximate=True).astype(jnp.bfloat16)
    result_rows = product(act_low, w_out[0]).astype(jnp.bfloat16).reshape(experts, capacity, width)
    returned = lax.all_to_all(
        result_rows, "expert", split_axis=0, concat_axis=0, tiled=True
    ).reshape(experts * capacity, width)
    expert_out = jnp.einsum("sq,sd->qd", placement, returned, preferred_element_type=jnp.float32)
    layer_out = (x_one + gate_value[:, None] * expert_out).astype(jnp.bfloat16)
    d_two = d_out[0].astype(jnp.float32)
    d_gate = jnp.sum(d_two * expert_out, axis=1)
    d_result = (gate_value[:, None] * d_two).astype(jnp.bfloat16)
    d_send = product(placement, d_result).astype(jnp.bfloat16).reshape(experts, capacity, width)
    d_received = lax.all_to_all(d_send, "expert", split_axis=0, concat_axis=0, tiled=True).reshape(
        experts * capacity, width
    )
    d_act = jnp.einsum("sd,fd->sf", d_received, w_out[0], preferred_element_type=jnp.float32)
    d_w_out_part = jnp.einsum("sf,sd->fd", act_low, d_received, preferred_element_type=jnp.float32)
    _, gelu_back = jax.vjp(lambda values_in: jax.nn.gelu(values_in, approximate=True), pre_act)
    d_pre = gelu_back(d_act)[0].astype(jnp.bfloat16)
    d_w_in_part = jnp.einsum("sd,sf->df", received, d_pre, preferred_element_type=jnp.float32)
    d_entry = (
        jnp.einsum("sf,df->sd", d_pre, w_in[0], preferred_element_type=jnp.float32)
        .astype(jnp.bfloat16)
        .reshape(experts, capacity, width)
    )
    d_back = lax.all_to_all(d_entry, "expert", split_axis=0, concat_axis=0, tiled=True).reshape(
        experts * capacity, width
    )
    d_h_two = jnp.einsum("sq,sd->qd", placement, d_back, preferred_element_type=jnp.float32)
    d_logits = router_probs * (chosen * d_gate[:, None] - (gate_value * d_gate)[:, None])
    d_router = jnp.dot(h_two_low.astype(jnp.float32).T, d_logits, precision=HIGHEST)
    d_h_two = d_h_two + jnp.dot(d_logits, router_all.astype(jnp.float32).T, precision=HIGHEST)
    d_x_part, d_gain_two = norm_backward(x_one, inverse_two, gain_two_f, d_h_two)
    d_x_one = d_two + d_x_part
    d_branch = d_x_one.astype(jnp.bfloat16)
    d_output = jnp.einsum("qi,qo->io", attn_low, d_branch, preferred_element_type=jnp.float32)
    d_attn = jnp.einsum(
        "qo,io->qi", d_branch, output_all, preferred_element_type=jnp.float32
    ).astype(jnp.bfloat16)
    d_attn_heads = d_attn.reshape(row_count, H, HD)
    row_delta = jnp.transpose(
        jnp.sum((d_attn.astype(jnp.float32) * mixed_rows).reshape(row_count, H, HD), axis=-1)
    )

    def query_core(d_query, key_block, value_block, ids_block, score_bias):
        scores = masked_scores(key_block, ids_block, score_bias)
        weights = jnp.exp(scores - log_total[..., None])
        value_heads = value_block.reshape(key_rows, H, HD)
        key_heads = key_block.reshape(key_rows, H, HD)
        d_weights = jnp.einsum(
            "qhd,khd->hqk", d_attn_heads, value_heads, preferred_element_type=jnp.float32
        )
        d_scores = weights * (d_weights - row_delta[..., None])
        d_raw = (d_scores * score_scale).astype(jnp.bfloat16)
        d_query = d_query + jnp.einsum(
            "hqk,khd->qhd", d_raw, key_heads, preferred_element_type=jnp.float32
        )
        return (d_query, weights, d_raw, d_scores)

    back_state = jnp.zeros((row_count, H, HD), jnp.float32)
    back_items = (key_blocks, value_blocks, ids_blocks, bias_blocks)

    def backward_step(d_query, item):
        key_block, value_block, ids_block, score_bias = item
        d_query, weights, d_raw, d_scores = query_core(
            d_query, key_block, value_block, ids_block, score_bias
        )
        d_key_block = jnp.einsum(
            "hqk,qhd->khd", d_raw, query_heads, preferred_element_type=jnp.float32
        ).reshape(key_rows, width)
        d_value_block = jnp.einsum(
            "hqk,qhd->khd",
            weights.astype(jnp.bfloat16),
            d_attn_heads,
            preferred_element_type=jnp.float32,
        ).reshape(key_rows, width)
        return (d_query, (jnp.concatenate([d_key_block, d_value_block], axis=1), d_scores))

    d_query, (pair_terms, score_grads) = lax.scan(backward_step, back_state, back_items)
    pair_sums = lax.psum_scatter(
        pair_terms.reshape(length, 2 * width).astype(jnp.bfloat16),
        "expert",
        scatter_dimension=0,
        tiled=True,
    ).astype(jnp.float32)
    d_key_low = pair_sums[:, :width].astype(jnp.bfloat16)
    d_value_low = pair_sums[:, width:].astype(jnp.bfloat16)
    score_grad_rows = jnp.transpose(score_grads, (1, 2, 0, 3)).reshape(H, row_count, length)
    d_offsets = bias_back(score_grad_rows)[0]
    d_query_low = d_query.reshape(row_count, width).astype(jnp.bfloat16)
    d_table = jnp.einsum("ob,ho->bh", bucket_hot, d_offsets, precision=HIGHEST)
    d_w_q = jnp.einsum("qi,qo->io", h_one_low, d_query_low, preferred_element_type=jnp.float32)
    d_w_k = jnp.einsum("qi,qo->io", h_one_low, d_key_low, preferred_element_type=jnp.float32)
    d_w_v = jnp.einsum("qi,qo->io", h_one_low, d_value_low, preferred_element_type=jnp.float32)
    d_h_one = jnp.einsum("qo,io->qi", d_query_low, query_all, preferred_element_type=jnp.float32)
    d_h_one = d_h_one + jnp.einsum(
        "qo,io->qi", d_key_low, key_all, preferred_element_type=jnp.float32
    )
    d_h_one = d_h_one + jnp.einsum(
        "qo,io->qi", d_value_low, value_all, preferred_element_type=jnp.float32
    )
    d_x_first, d_gain_one = norm_backward(flat_rows, inverse_one, gain_one_f, d_h_one)
    d_tokens = (d_x_one + d_x_first)[None]
    shard_q, shard_k, shard_v, shard_o, shard_router, shard_one, shard_two, shard_table = (
        lax.psum_scatter(
            d_w_q.astype(jnp.bfloat16), "shard", scatter_dimension=0, tiled=True
        ).astype(jnp.float32),
        lax.psum_scatter(
            d_w_k.astype(jnp.bfloat16), "shard", scatter_dimension=0, tiled=True
        ).astype(jnp.float32),
        lax.psum_scatter(
            d_w_v.astype(jnp.bfloat16), "shard", scatter_dimension=0, tiled=True
        ).astype(jnp.float32),
        lax.psum_scatter(
            d_output.astype(jnp.bfloat16), "shard", scatter_dimension=0, tiled=True
        ).astype(jnp.float32),
        lax.psum_scatter(
            d_router.astype(jnp.bfloat16), "shard", scatter_dimension=0, tiled=True
        ).astype(jnp.float32),
        lax.psum_scatter(
            d_gain_one.astype(jnp.bfloat16), "shard", scatter_dimension=0, tiled=True
        ).astype(jnp.float32),
        lax.psum_scatter(
            d_gain_two.astype(jnp.bfloat16), "shard", scatter_dimension=0, tiled=True
        ).astype(jnp.float32),
        lax.psum_scatter(
            d_table.astype(jnp.bfloat16), "shard", scatter_dimension=0, tiled=True
        ).astype(jnp.float32),
    )
    total_q, total_k, total_v, total_o, total_router, total_one, total_two, total_table = (
        lax.psum(shard_q.astype(jnp.bfloat16), "expert").astype(jnp.float32),
        lax.psum(shard_k.astype(jnp.bfloat16), "expert").astype(jnp.float32),
        lax.psum(shard_v.astype(jnp.bfloat16), "expert").astype(jnp.float32),
        lax.psum(shard_o.astype(jnp.bfloat16), "expert").astype(jnp.float32),
        lax.psum(shard_router.astype(jnp.bfloat16), "expert").astype(jnp.float32),
        lax.psum(shard_one.astype(jnp.bfloat16), "expert").astype(jnp.float32),
        lax.psum(shard_two.astype(jnp.bfloat16), "expert").astype(jnp.float32),
        lax.psum(shard_table.astype(jnp.bfloat16), "expert").astype(jnp.float32),
    )
    grad_in, grad_out = (
        lax.psum_scatter(
            d_w_in_part[None].astype(jnp.bfloat16), "shard", scatter_dimension=1, tiled=True
        ).astype(jnp.float32),
        lax.psum_scatter(
            d_w_out_part[None].astype(jnp.bfloat16), "shard", scatter_dimension=1, tiled=True
        ).astype(jnp.float32),
    )
    return (
        layer_out[None],
        d_tokens,
        total_q,
        total_k,
        total_v,
        total_o,
        total_router,
        total_one,
        total_two,
        total_table,
        grad_in,
        grad_out,
    )


def solution(mesh):
    placed = (
        P("shard", "expert", None),
        P("shard", None),
        P("shard", None),
        P("shard", None),
        P("shard", None),
        P("shard", None),
        P("shard"),
        P("shard"),
        P("shard", None),
        P("expert", None, None),
        P("expert", None, None),
        P("shard", "expert", None),
        P("shard", None),
        P(),
        P("shard", "expert", None),
    )
    return jax.shard_map(
        per_device,
        mesh=mesh,
        in_specs=placed,
        out_specs=(
            P("shard", "expert", None),
            P("shard", "expert", None),
            P("shard", None),
            P("shard", None),
            P("shard", None),
            P("shard", None),
            P("shard", None),
            P("shard"),
            P("shard"),
            P("shard", None),
            P("expert", "shard", None),
            P("expert", "shard", None),
        ),
        check_vma=False,
    )
```

profile of v0, /device:TPU:0, one launch (start us, length us, event | category | flops | bytes accessed | tf_op | source)
XLA Modules:
  0.0 1066.5 jit_solution(1404222445242232202)
XLA Ops:
  13.1 23.1 %all-reduce.9 = (bf16[768]{0:T(1024)(128)(2,1)S(1)}, bf16[768]{0:T(1024)(128)(2,1)S(1)}) all-reduce(bf16[768]{0:T(1024)(128)(2,1)S(1)} %dynamic-update-slice, bf16[768]{0:T(1024)(128)(2,1)S(1)} %dynamic-update-slice.1), channel_id=1, replica_groups=mesh['expert'=4,'shard'=8] {'shard'}, use_global_device_ids=true, to_apply=%add.3 | all-reduce | flops 1536 | bytes 6144
  38.0 15.9 %all-gather.13.cloned.1.call-done = bf16[768,768]{1,0:T(8,128)(2,1)} async-done(((bf16[96,768]{1,0:T(8,128)(2,1)}), bf16[768,768]{1,0:T(8,128)(2,1)}) %all-gather.13.cloned.1.call-update) | async-done | bytes 1179664 | tf_op jit(solution)/shard_map/all_gather | solution.py:71
  56.7 39.3 %all-gather.9.cloned.1.call-done = bf16[768,768]{1,0:T(8,128)(2,1)} async-done(((bf16[96,768]{1,0:T(8,128)(2,1)}), bf16[768,768]{1,0:T(8,128)(2,1)}) %all-gather.9.cloned.1.call-update) | async-done | bytes 1179664 | tf_op jit(solution)/shard_map/all_gather | solution.py:72
  99.3 18.3 %all-gather = bf16[8,4,12]{2,1,0:T(4,128)(2,1)S(1)} all-gather(bf16[1,4,12]{2,1,0:T(4,128)(2,1)S(1)} %bitcast.314), channel_id=1, replica_groups=mesh['expert'=4,'shard'=8] {'shard'}, dimensions={0}, use_global_device_ids=true | all-gather | bytes 864 | tf_op jit(solution)/shard_map/all_gather | solution.py:77
  121.5 14.4 %copy.127 = f32[2,8,256,1280]{3,1,2,0:T(8,128)} copy(f32[2,8,256,1280]{3,2,1,0:T(8,128)S(1)} %bitcast.275) | data formatting | bytes 41943040
  135.9 15.7 %slice.27 = f32[12,327424]{1,0:T(8,128)} slice(f32[12,327680]{1,0:T(8,128)} %bitcast.277), slice={[0:12], [0:327424]} | slice | bytes 31432704 | tf_op jit(solution)/shard_map/jvp()/slice | solution.py:38
  151.6 31.3 %reshape.270 = f32[12,256,1279]{2,1,0:T(8,128)} reshape(f32[12,327424]{1,0:T(8,128)} %slice.27) | data formatting | bytes 31432704 | tf_op jit(solution)/shard_map/jvp()/reshape | solution.py:38
  182.9 12.9 %slice.28 = f32[12,256,1024]{2,1,0:T(8,128)} slice(f32[12,256,1279]{2,1,0:T(8,128)} %reshape.270), slice={[0:12], [0:256], [255:1279]} | slice | bytes 25165824 | tf_op jit(solution)/shard_map/jvp()/slice | solution.py:41
  195.8 12.6 %copy.85 = f32[12,256,1024]{1,2,0:T(8,128)} copy(f32[12,256,1024]{2,1,0:T(8,128)} %slice.28) | data formatting | bytes 25165824 | tf_op jit(solution)/shard_map/jvp()/slice | solution.py:41
  208.4 10.4 copy.87
  220.0 16.6 %all-gather.1 = bf16[8,96,4]{1,2,0:T(4,128)(2,1)S(1)} all-gather(bf16[1,96,4]{1,2,0:T(4,128)(2,1)S(1)} %bitcast.315), channel_id=1, replica_groups=mesh['expert'=4,'shard'=8] {'shard'}, dimensions={0}, use_global_device_ids=true | all-gather | bytes 6912 | tf_op jit(solution)/shard_map/all_gather | solution.py:74
  242.8 30.2 %while.41 = (s32[]{:T(128)}, f32[12,256]{1,0:T(8,128)S(1)}, f32[12,256]{1,0:T(8,128)S(1)}, f32[2,12,256,512]{2,3,1,0:T(8,128)}, s32[256]{0:T(256)S(1)}, /*index=...) while((s32[]{:T(128)}, f32[12,256]{1,0:T(8,128)S(1)}, ...), condition=%wide.region_4.5_spmd.clone, body=%wide.region_1.4_spmd.clone.sunk | while | flops 210910208 | bytes 59805344 | solution.py:135
  243.0 6.8 fusion.177
  258.1 6.8 fusion.177
  276.2 34.6 %while.42 = (s32[]{:T(128)}, f32[256,12,64]{0,2,1:T(8,128)S(1)}, bf16[2,512,768]{1,2,0:T(8,128)(2,1)}, f32[2,12,256,512]{2,3,1,0:T(8,128)}, f32[12,256]{1,0:T(8,128)S(1)}, /*index=5*/s32[]{:T(128)}, s32[]{:T(128)}) while((s32[]{:T(128)}, f32[256,12,64]{0,2,1:T(8,128)S(1)}, bf16[2,512,768]{1,2,0:T(8,128)(2,1)}, ...), condition=%wide.region_6.7_spmd.clone, body=%wide.region_5.6_spmd.clone.sunk | while | flops 204865536 | bytes 35401820 | solution.py:150
  276.2 5.8 constant_dynamic-slice_fusion.18
  282.0 6.6 copy.133
  293.5 5.8 constant_dynamic-slice_fusion.18
  299.3 6.6 copy.133
  323.8 6.2 all-to-all-done
  334.2 4.6 fusion.35
  341.6 4.7 fusion.44
  346.2 9.8 fusion.28
  360.2 6.8 fusion.41
  367.1 4.8 all-to-all-done.1
  379.9 8.0 all-to-all-done.3
  397.4 52.7 %while.43 = (s32[]{:T(128)}, f32[256,12,64]{0,2,1:T(8,128)}, bf16[2,512,1536]{2,1,0:T(8,128)(2,1)}, f32[2,12,256,512]{2,3,0,1:T(8,128)}, bf16[2,512,768]{1,2,0:T...) while((s32[]{:T(128)}, f32[256,12,64]{0,2,1:T(8,128)}, ...), condition=%wide.region_18.19_spmd.clone, body=%wide.region_17.18_spmd.clone.sunk | while | flops 1027604480 | bytes 199364464 | solution.py:253
  400.8 4.7 fusion.190
  419.4 4.3 fusion.191
  426.9 4.7 fusion.190
  445.5 4.5 fusion.191
  457.1 28.5 %reduce-scatter.11.cloned.1.call-done = bf16[256,1536]{1,0:T(8,128)(2,1)} async-done(((bf16[1024,1536]{1,0:T(8,128)(2,1)}), bf16[256,1536]{1,0:T(8,128)(2,1)}) %reduce-scatter.11.cloned.1.call-update) | async-done | bytes 786448 | tf_op jit(solution)/shard_map/reduce_scatter | solution.py:254
  491.0 8.4 fusion.38
  499.5 6.6 fusion.37
  507.5 12.7 %copy.126 = f32[12,256,1024]{2,1,0:T(8,128)} copy(f32[12,256,1024]{1,2,0:T(8,128)} %bitcast.289) | data formatting | bytes 25165824
  520.2 13.9 %pad.16.clone = f32[12,256,1279]{2,1,0:T(8,128)} pad(f32[12,256,1024]{2,1,0:T(8,128)} %copy.126, f32[]{:T(128)} %constant.60.clone.1), padding=0_0x0_0x255_0 | pad | bytes 28299268 | tf_op jit(solution)/shard_map/transpose(jvp())/pad | solution.py:41
  534.1 25.2 %reshape.285 = f32[12,327424]{1,0:T(8,128)} reshape(f32[12,256,1279]{2,1,0:T(8,128)} %pad.16.clone) | data formatting | bytes 31432704 | tf_op jit(solution)/shard_map/transpose(jvp())/reshape | solution.py:38
  559.3 8.0 pad.17
  567.3 10.4 copy.129
  577.7 6.5 slice_reduce_fusion
  593.3 37.2 %all-reduce.8 = (bf16[768]{0:T(1024)(128)(2,1)S(1)}, bf16[768]{0:T(1024)(128)(2,1)S(1)}, bf16[32,12]{1,0:T(8,128)(2,1)S(1)}) all-reduce(bf16[768]{0:T(1024)(128)(2,1)S(1)} %get-tuple-element.364, bf16[768]{0:T(1024)(128)(2,1)S(1)} %copy-done.47, ...), channel_id=8, replica_groups=mesh['expert'=4,'shard'=8] {'shard'}, use_global_device_ids=true, to_apply=%region_32.33.clone | all-reduce | flops 1920 | bytes 7680
  630.7 54.6 %reduce-scatter.13.cloned.1.call-done = bf16[96,768]{1,0:T(8,128)(2,1)} async-done(((bf16[768,768]{1,0:T(8,128)(2,1)}), bf16[96,768]{1,0:T(8,128)(2,1)}) %reduce-scatter.13.cloned.1.call-update) | async-done | bytes 147472 | tf_op jit(solution)/shard_map/reduce_scatter | solution.py:279
  685.3 67.4 %reduce-scatter.15.cloned.1.call-done = bf16[96,768]{1,0:T(8,128)(2,1)} async-done(((bf16[768,768]{1,0:T(8,128)(2,1)}), bf16[96,768]{1,0:T(8,128)(2,1)}) %reduce-scatter.15.cloned.1.call-update) | async-done | bytes 147472 | tf_op jit(solution)/shard_map/reduce_scatter | solution.py:282
  752.7 66.7 %reduce-scatter.17.cloned.1.call-done = bf16[96,768]{1,0:T(8,128)(2,1)} async-done(((bf16[768,768]{1,0:T(8,128)(2,1)}), bf16[96,768]{1,0:T(8,128)(2,1)}) %reduce-scatter.17.cloned.1.call-update) | async-done | bytes 147472 | tf_op jit(solution)/shard_map/reduce_scatter | solution.py:285
  819.4 5.8 all-reduce.10
  828.5 89.3 %reduce-scatter.23.cloned.1.call-done = bf16[1,384,768]{2,1,0:T(8,128)(2,1)} async-done(((bf16[1,3072,768]{2,1,0:T(8,128)(2,1)}), bf16[1,384,768]{2,1,0:T(8,128)(2,1)}) %reduce-scatter.23.cloned.1.call-update) | async-done | bytes 589840 | tf_op jit(solution)/shard_map/reduce_scatter | solution.py:318
  920.0 97.0 %reduce-scatter.21.cloned.1.call-done = bf16[1,96,3072]{2,1,0:T(8,128)(2,1)} async-done(((bf16[1,768,3072]{2,1,0:T(8,128)(2,1)}), bf16[1,96,3072]{2,1,0:T(8,128)(2,1)}) %reduce-scatter.21.cloned.1.call-update) | async-done | bytes 589840 | tf_op jit(solution)/shard_map/reduce_scatter | solution.py:315
  1019.2 34.1 %all-reduce.14.cloned.1.call-done = (bf16[96,768]{1,0:T(8,128)(2,1)}, bf16[96,768]{1,0:T(8,128)(2,1)}, bf16[96,768]{1,0:T(8,128)(2,1)}, bf16[96,768]{1,0:T(8,128)(2,1)}) async-done(((bf16[96,768]{1,0:T(8,128)(2,1)}, bf16[96,768]{1,0:T(8,128)(2,1)}, bf16[96,768]{1,0:T(8,128)(2,1)}, bf16[96,768]{1,0:T(8,128)(2,1)}), (bf16[96,768]{1,0:T(8,128)(2,1)}, bf16[96,768]{1,0:T(8,128)(2,1)}, bf16[96,768]{1,0:T(8,128)(2,1)}, ...) | async-done | bytes 589840 | tf_op jit(solution)/shard_map/psum | solution.py:305
  (302 shorter events, 164.5 us)
Async XLA Ops:
  7.2 92.2 %copy-start.51 = (bf16[4,12]{1,0:T(4,128)(2,1)S(1)}, bf16[4,12]{1,0:T(4,128)(2,1)}, u32[]{:S(2)}) copy-start(bf16[4,12]{1,0:T(4,128)(2,1)} %param.29) | copy-start | bytes 292
  7.2 110.5 %copy-start.53 = (s32[2047]{0:T(1024)S(1)}, s32[2047]{0:T(1024)}, u32[]{:S(2)}) copy-start(s32[2047]{0:T(1024)} %param.34) | copy-start | bytes 24568
  7.2 46.8 %all-gather.13.cloned.1.call-start = ((), (), s32[]{:S(2)}) async-start(), calls=%async_computation.14 | async-start | bytes 1327104 | tf_op jit(solution)/shard_map/all_gather | solution.py:71
  7.9 88.1 %all-gather.9.cloned.1.call-start = ((), (), s32[]{:S(2)}) async-start(), calls=%async_computation.12 | async-start | bytes 1327104 | tf_op jit(solution)/shard_map/all_gather | solution.py:72
  8.7 230.3 %all-gather.17.cloned.1.call-start = ((), (), s32[]{:S(2)}) async-start(), calls=%async_computation.16 | async-start | bytes 1327104 | tf_op jit(solution)/shard_map/all_gather | solution.py:70
  9.4 231.6 %all-gather.15.cloned.1.call-start = ((), (), s32[]{:S(2)}) async-start(), calls=%async_computation.15 | async-start | bytes 1966080 | tf_op jit(solution)/shard_map/all_gather | solution.py:94
  36.3 202.7 %copy-start.26 = (f32[768]{0:T(1024)}, f32[768]{0:T(1024)S(1)}, u32[]{:S(2)}) copy-start(f32[768]{0:T(1024)S(1)} %convert_element_type.203) | copy-start | bytes 9220
  38.0 201.0 %copy-start.37 = (f32[256]{0:T(256)}, f32[256]{0:T(256)S(1)}, u32[]{:S(2)}) copy-start(f32[256]{0:T(256)S(1)} %get-tuple-element.442) | copy-start | bytes 3076
  56.7 216.3 %all-gather.11.cloned.1.call-start = ((), (), s32[]{:S(2)}) async-start(), calls=%async_computation.13 | async-start | bytes 1966080 | tf_op jit(solution)/shard_map/all_gather | solution.py:95
  98.7 212.1 %all-gather.19.cloned.1.call-start = ((), (), s32[]{:S(2)}) async-start(), calls=%async_computation.17 | async-start | bytes 1327104 | tf_op jit(solution)/shard_map/all_gather | solution.py:73
  208.4 11.6 %copy-start.52 = (bf16[96,4]{0,1:T(4,128)(2,1)S(1)}, bf16[96,4]{0,1:T(4,128)(2,1)}, u32[]{:S(2)}) copy-start(bf16[96,4]{0,1:T(4,128)(2,1)} %param.26) | copy-start | bytes 2308
  208.4 29.0 %copy-start.31 = (s32[1,256,1]{1,2,0:T(1,128)S(1)}, s32[1,256,1]{1,2,0:T(1,128)}, u32[]{:S(2)}) copy-start(s32[1,256,1]{1,2,0:T(1,128)} %param.32) | copy-start | bytes 3076
  208.4 30.7 %copy-start.10 = (bf16[1,256,768]{2,1,0:T(8,128)(2,1)S(1)}, bf16[1,256,768]{2,1,0:T(8,128)(2,1)}, u32[]{:S(2)}) copy-start(bf16[1,256,768]{2,1,0:T(8,128)(2,1)} %param.21) | copy-start | bytes 1179652
  220.0 93.3 %copy-start.28 = (f32[768]{0:T(1024)}, f32[768]{0:T(1024)S(1)}, u32[]{:S(2)}) copy-start(f32[768]{0:T(1024)S(1)} %convert_element_type.209) | copy-start | bytes 9220
  239.0 74.4 %copy-start.35 = (s32[256]{0:T(256)}, s32[256]{0:T(256)S(1)}, u32[]{:S(2)}) copy-start(s32[256]{0:T(256)S(1)} %multiply_add_fusion) | copy-start | bytes 3076
  310.8 11.0 %copy-start.14 = (bf16[1,256,768]{2,1,0:T(8,128)(2,1)S(1)}, bf16[1,256,768]{2,1,0:T(8,128)(2,1)}, u32[]{:S(2)}) copy-start(bf16[1,256,768]{2,1,0:T(8,128)(2,1)} %param.35) | copy-start | bytes 1179652
  313.4 25.4 %copy-start.13 = (bf16[256,768]{1,0:T(8,128)(2,1)}, bf16[256,768]{1,0:T(8,128)(2,1)S(1)}, u32[]{:S(2)}) copy-start(bf16[256,768]{1,0:T(8,128)(2,1)S(1)} %multiply_convert_fusion.4) | copy-start | bytes 1179652
  314.7 15.3 %all-to-all-start = ((bf16[4,128,768]{2,1,0:T(8,128)(2,1)}), bf16[4,128,768]{2,1,0:T(8,128)(2,1)S(1)}, u32[]{:S(2)}, u32[]{:S(2)}) async-start(bf16[4,128,768]{2,1,0:T(8,128)(2,1)} %bitcast.297), calls=%async_computation | async-start | bytes 1572864 | tf_op jit(solution)/shard_map/all_to_all | solution.py:172
  330.0 16.2 %all-to-all-start.2 = ((bf16[4,128,768]{2,1,0:T(8,128)(2,1)}), bf16[4,128,768]{2,1,0:T(8,128)(2,1)}, u32[]{:S(2)}, u32[]{:S(2)}) async-start(bf16[4,128,768]{2,1,0:T(8,128)(2,1)} %bitcast.295), calls=%async_computation.2 | async-start | bytes 1572864 | tf_op jit(solution)/shard_map/all_to_all | solution.py:187
  356.0 15.9 %all-to-all-start.1 = ((bf16[4,128,768]{2,1,0:T(8,128)(2,1)}), bf16[4,128,768]{2,1,0:T(8,128)(2,1)}, u32[]{:S(2)}, u32[]{:S(2)}) async-start(bf16[4,128,768]{2,1,0:T(8,128)(2,1)} %bitcast.21), calls=%async_computation.1 | async-start | bytes 1572864 | tf_op jit(solution)/shard_map/all_to_all | solution.py:178
  360.2 17.2 %copy-start.36 = (s32[256]{0:T(256)S(1)}, s32[256]{0:T(256)}, u32[]{:S(2)}) copy-start(s32[256]{0:T(256)} %copy-done.35) | copy-start | bytes 3076
  360.2 19.6 %copy-start.45 = (f32[256]{0:T(256)S(1)}, f32[256]{0:T(256)}, u32[]{:S(2)}) copy-start(f32[256]{0:T(256)} %copy-done.44) | copy-start | bytes 3076
  367.1 22.4 %copy-start.25 = (f32[256,4]{0,1:T(4,128)S(1)}, f32[256,4]{0,1:T(4,128)}, u32[]{:S(2)}) copy-start(f32[256,4]{0,1:T(4,128)} %copy-done.24) | copy-start | bytes 12292
  367.1 22.4 %copy-start.29 = (f32[768]{0:T(1024)S(1)}, f32[768]{0:T(1024)}, u32[]{:S(2)}) copy-start(f32[768]{0:T(1024)} %copy-done.28) | copy-start | bytes 9220
  367.1 22.4 %copy-start.30 = (bf16[768,4]{0,1:T(4,128)(2,1)S(1)}, bf16[768,4]{0,1:T(4,128)(2,1)}, u32[]{:S(2)}) copy-start(bf16[768,4]{0,1:T(4,128)(2,1)} %reshape.298) | copy-start | bytes 18436
  367.1 22.4 %copy-start.32 = (s32[1,256,1]{1,2,0:T(1,128)S(1)}, s32[1,256,1]{1,2,0:T(1,128)}, u32[]{:S(2)}) copy-start(s32[1,256,1]{1,2,0:T(1,128)} %param.32) | copy-start | bytes 3076
  367.1 22.4 %copy-start.34 = (f32[256]{0:T(256)S(1)}, f32[256]{0:T(256)}, u32[]{:S(2)}) copy-start(f32[256]{0:T(256)} %copy-done.33) | copy-start | bytes 3076
  367.1 22.4 %copy-start.41 = (f32[256]{0:T(256)S(1)}, f32[256]{0:T(256)}, u32[]{:S(2)}) copy-start(f32[256]{0:T(256)} %copy-done.40) | copy-start | bytes 3076
  367.1 22.4 %copy-start.43 = (f32[256]{0:T(256)S(1)}, f32[256]{0:T(256)}, u32[]{:S(2)}) copy-start(f32[256]{0:T(256)} %copy-done.42) | copy-start | bytes 3076
  367.1 23.7 %copy-start.15 = (bf16[1,256,768]{2,1,0:T(8,128)(2,1)S(1)}, bf16[1,256,768]{2,1,0:T(8,128)(2,1)}, u32[]{:S(2)}) copy-start(bf16[1,256,768]{2,1,0:T(8,128)(2,1)} %param.35) | copy-start | bytes 1179652
  367.1 23.7 %copy-start.50 = (f32[256]{0:T(256)S(1)}, f32[256]{0:T(256)}, u32[]{:S(2)}) copy-start(f32[256]{0:T(256)} %get-tuple-element.443) | copy-start | bytes 3076
  371.9 15.9 %all-to-all-start.3 = ((bf16[4,128,768]{2,1,0:T(8,128)(2,1)}), bf16[4,128,768]{2,1,0:T(8,128)(2,1)}, u32[]{:S(2)}, u32[]{:S(2)}) async-start(bf16[4,128,768]{2,1,0:T(8,128)(2,1)} %bitcast.300), calls=%async_computation.3 | async-start | bytes 1572864 | tf_op jit(solution)/shard_map/all_to_all | solution.py:200
  376.1 109.5 %reduce-scatter.11.cloned.1.call-start = ((), (), s32[]{:S(2)}) async-start(), calls=%async_computation.18 | async-start | bytes 3932160 | tf_op jit(solution)/shard_map/reduce_scatter | solution.py:254
  379.8 13.2 %copy-start.39 = (f32[256]{0:T(256)}, f32[256]{0:T(256)S(1)}, u32[]{:S(2)}) copy-start(f32[256]{0:T(256)S(1)} %get-tuple-element.451) | copy-start | bytes 3076
  379.8 13.2 %copy-start.46 = (f32[256]{0:T(256)}, f32[256]{0:T(256)S(1)}, u32[]{:S(2)}) copy-start(f32[256]{0:T(256)S(1)} %mul.321) | copy-start | bytes 3076
  397.6 12.1 %copy-start.3 = (bf16[256,12,64]{0,2,1:T(8,128)(2,1)}, bf16[256,12,64]{0,2,1:T(8,128)(2,1)S(1)}, u32[]{:S(2)}) copy-start(bf16[256,12,64]{0,2,1:T(8,128)(2,1)S(1)} %get-tuple-element.729) | copy-start | bytes 1179652 | tf_op jit(solution)/shard_map/while
  423.7 12.1 %copy-start.3 = (bf16[256,12,64]{0,2,1:T(8,128)(2,1)}, bf16[256,12,64]{0,2,1:T(8,128)(2,1)S(1)}, u32[]{:S(2)}) copy-start(bf16[256,12,64]{0,2,1:T(8,128)(2,1)S(1)} %get-tuple-element.729) | copy-start | bytes 1179652 | tf_op jit(solution)/shard_map/while
  450.1 138.2 %reduce-scatter.25.cloned.1.call-start = ((), (), s32[]{:S(2)}) async-start(), calls=%async_computation.25 | async-start | bytes 221184
  452.4 178.3 %reduce-scatter.19.cloned.1.call-start = ((), (), s32[]{:S(2)}) async-start(), calls=%async_computation.22 | async-start | bytes 1327104 | tf_op jit(solution)/shard_map/reduce_scatter | solution.py:288
  455.3 230.0 %reduce-scatter.13.cloned.1.call-start = ((), (), s32[]{:S(2)}) async-start(), calls=%async_computation.19 | async-start | bytes 1327104 | tf_op jit(solution)/shard_map/reduce_scatter | solution.py:279
  457.0 295.7 %reduce-scatter.15.cloned.1.call-start = ((), (), s32[]{:S(2)}) async-start(), calls=%async_computation.20 | async-start | bytes 1327104 | tf_op jit(solution)/shard_map/reduce_scatter | solution.py:282
  488.2 331.1 %reduce-scatter.17.cloned.1.call-start = ((), (), s32[]{:S(2)}) async-start(), calls=%async_computation.21 | async-start | bytes 1327104 | tf_op jit(solution)/shard_map/reduce_scatter | solution.py:285
  491.0 426.9 %reduce-scatter.23.cloned.1.call-start = ((), (), s32[]{:S(2)}) async-start(), calls=%async_computation.24 | async-start | bytes 5308416 | tf_op jit(solution)/shard_map/reduce_scatter | solution.py:318
  499.5 517.5 %reduce-scatter.21.cloned.1.call-start = ((), (), s32[]{:S(2)}) async-start(), calls=%async_computation.23 | async-start | bytes 5308416 | tf_op jit(solution)/shard_map/reduce_scatter | solution.py:315
  506.2 547.1 %all-reduce.14.cloned.1.call-start = ((), (), s32[]{:S(2)}) async-start(), calls=%async_computation.26 | async-start | bytes 1179648 | tf_op jit(solution)/shard_map/psum | solution.py:305
  577.7 12.0 %copy-start.19 = (bf16[768,768]{1,0:T(8,128)(2,1)S(1)}, bf16[768,768]{1,0:T(8,128)(2,1)}, u32[]{:S(2)}) copy-start(bf16[768,768]{1,0:T(8,128)(2,1)} %all-gather.13.cloned.1.call-done) | copy-start | bytes 3538948
  584.3 243.1 %copy-start.9 = (f32[256,768]{1,0:T(8,128)S(1)}, f32[256,768]{1,0:T(8,128)}, u32[]{:S(2)}) copy-start(f32[256,768]{1,0:T(8,128)} %copy-done.8) | copy-start | bytes 2359300
  584.3 243.1 %copy-start.49 = (f32[256]{0:T(256)S(1)}, f32[256]{0:T(256)}, u32[]{:S(2)}) copy-start(f32[256]{0:T(256)} %get-tuple-element.441) | copy-start | bytes 3076
  (36 other events, 189.9 us)
Sparse Core Ops, SparseCore 0:
  10.2 43.7 all-gather.12
  56.2 39.8 all-gather.8
  98.2 39.8 all-gather.16
  140.1 18.4 all-gather.14
  160.5 19.6 all-gather.10
  182.2 41.0 all-gather.18
  450.2 35.3 reduce-scatter.10
  489.8 61.0 reduce-scatter.24
  554.7 63.1 reduce-scatter.18
  622.0 63.1 reduce-scatter.12
  689.6 63.0 reduce-scatter.14
  756.3 63.0 reduce-scatter.16
  823.5 94.3 reduce-scatter.22
  921.8 95.1 reduce-scatter.20
  1019.6 33.6 all-reduce.13
where the time goes:
time: 1080 us; the launch traced here: 1070 us
  waiting for transfers between devices  515 us (48%)
  local copies, waits for them, and re-layouts  251 us (23%)
  matrix products  127 us (12%)
  blocking collectives  101 us (9%)
  other arithmetic  38 us (4%)
  between operations  16.9 us (2%)
  starting transfers between devices  16.8 us (2%)
    reduce_scatter x1, waiting for transfers between devices, per_device(): lax.psum_scatter(d_w_in_part[None].astype(jnp.bfloat16), 'shard', scatter...  97 us
    reduce_scatter x1, waiting for transfers between devices, per_device(): lax.psum_scatter(d_w_out_part[None].astype(jnp.bfloat16), 'shard', scatte...  89.3 us
    reduce_scatter x1, waiting for transfers between devices, per_device(): lax.psum_scatter(d_w_k.astype(jnp.bfloat16), 'shard', scatter_dimension=0...  67.4 us
    reduce_scatter x1, waiting for transfers between devices, per_device(): lax.psum_scatter(d_w_v.astype(jnp.bfloat16), 'shard', scatter_dimension=0...  66.7 us
    unnamed x117, local copies, waits for them, and re-layouts  65.6 us
    unnamed x2, blocking collectives  60.4 us
    reshape x2, local copies, waits for them, and re-layouts, skew_bias(): tiled_rows[:, :row_count * span_width]  56.5 us
    reduce_scatter x1, waiting for transfers between devices, per_device(): lax.psum_scatter(d_w_q.astype(jnp.bfloat16), 'shard', scatter_dimension=0...  54.6 us
  transfers between devices with their start and end apart: 19, of which 12 were waited for; matrix products, arithmetic and copies ran while one was open for 31% of the time, Pallas kernels for 0%

commit v1 on v0

v1 whole, which is shorter than its diff:
```python
import jax
import jax.numpy as jnp
from jax import lax
from jax.experimental import pallas as pl
from jax.experimental.pallas import tpu as pltpu
from jax.sharding import PartitionSpec as P

H = 12
HD = 64

EPSILON = 1e-06
NEGATIVE = -1e30
HIGHEST = lax.Precision.HIGHEST


def product(left, right):
    return jnp.dot(left, right, preferred_element_type=jnp.float32)


def contract(left, right, left_dim, right_dim):
    return lax.dot_general(
        left, right, (((left_dim,), (right_dim,)), ((), ())), preferred_element_type=jnp.float32
    )


def norm_forward(values_in, gain):
    inverse = lax.rsqrt(jnp.mean(values_in * values_in, axis=-1, keepdims=True) + EPSILON)
    return (values_in * inverse * gain, inverse)


def norm_backward(values_in, inverse, gain, grad_in):
    scaled = grad_in * gain
    inner_mean = jnp.mean(scaled * values_in, axis=-1, keepdims=True)
    grad_out = inverse * scaled - values_in * (inverse * inverse * inverse) * inner_mean
    gain_grad = jnp.sum(grad_in * values_in * inverse, axis=0)
    return (grad_out, gain_grad)


def round_up(count, step):
    return -(-count // step) * step


def block_scores(query_ref, key_ref, row_ids_ref, col_ids_ref, window_ref):
    rows = query_ref.shape[1]
    length = key_ref.shape[1]
    span = window_ref.shape[3]
    spread = jnp.broadcast_to(window_ref[0, 0], (rows, span))
    bias = pltpu.roll(spread, span - (rows - 1), 1, stride=1, stride_axis=0)[:, :length]
    scores = contract(query_ref[0], key_ref[0], 1, 1) + bias
    return jnp.where(row_ids_ref[...] == col_ids_ref[...], scores, NEGATIVE)


def forward_kernel(
    query_ref, key_ref, value_ref, row_ids_ref, col_ids_ref, window_ref, mixed_ref, log_ref
):
    scores = block_scores(query_ref, key_ref, row_ids_ref, col_ids_ref, window_ref)
    peak = jnp.max(scores, axis=1, keepdims=True)
    powers = jnp.exp(scores - peak)
    total = jnp.sum(powers, axis=1, keepdims=True)
    weights = (powers * (1.0 / total)).astype(jnp.bfloat16)
    mixed_ref[0] = contract(weights, value_ref[0], 1, 0)
    log_ref[0] = peak + jnp.log(total)


def backward_kernel(
    query_ref,
    key_ref,
    value_ref,
    row_ids_ref,
    col_ids_ref,
    window_ref,
    mixed_ref,
    log_ref,
    d_mixed_ref,
    d_query_ref,
    d_key_ref,
    d_value_ref,
    d_window_ref,
):
    rows = query_ref.shape[1]
    length = key_ref.shape[1]
    span = window_ref.shape[3]

    @pl.when(pl.program_id(1) == 0)
    def _():
        d_key_ref[...] = jnp.zeros_like(d_key_ref)
        d_value_ref[...] = jnp.zeros_like(d_value_ref)

    scores = block_scores(query_ref, key_ref, row_ids_ref, col_ids_ref, window_ref)
    weights = jnp.exp(scores - log_ref[0])
    d_mixed = d_mixed_ref[0]
    delta = jnp.sum(d_mixed.astype(jnp.float32) * mixed_ref[0], axis=1, keepdims=True)
    d_scores = weights * (contract(d_mixed, value_ref[0], 1, 1) - delta)
    d_low = d_scores.astype(jnp.bfloat16)
    d_query_ref[0] = (contract(d_low, key_ref[0], 1, 0) * (HD**-0.5)).astype(jnp.bfloat16)
    d_key_ref[0] += contract(d_low, query_ref[0], 0, 0)
    d_value_ref[0] += contract(weights.astype(jnp.bfloat16), d_mixed, 0, 0)
    folded = jnp.concatenate(
        [d_scores, jnp.zeros((rows, span - length), jnp.float32)], axis=1
    )
    half = rows // 2
    while half >= 8:
        folded = pltpu.roll(folded[:half], half, 1) + folded[half:]
        half //= 2
    d_window_ref[0, 0] = folded


def attention_specs(heads, blocks, rows, length, span):
    per_block = pl.BlockSpec((1, rows, HD), lambda h, i: (h, i, 0))
    per_head = pl.BlockSpec((1, length, HD), lambda h, i: (h, 0, 0))
    row_ids = pl.BlockSpec((rows, 1), lambda h, i: (i, 0))
    col_ids = pl.BlockSpec((1, length), lambda h, i: (0, 0))
    window = pl.BlockSpec((1, 1, 1, span), lambda h, i: (h, i, 0, 0))
    logs = pl.BlockSpec((1, rows, 1), lambda h, i: (h, i, 0))
    return per_block, per_head, row_ids, col_ids, window, logs


def attention_forward(query, key, value, row_ids, col_ids, windows):
    heads, length, _ = query.shape
    blocks, span = windows.shape[1], windows.shape[3]
    rows = length // blocks
    per_block, per_head, rid, cid, window, logs = attention_specs(
        heads, blocks, rows, length, span
    )
    return pl.pallas_call(
        forward_kernel,
        grid=(heads, blocks),
        in_specs=[per_block, per_head, per_head, rid, cid, window],
        out_specs=[per_block, logs],
        out_shape=[
            jax.ShapeDtypeStruct((heads, length, HD), jnp.float32),
            jax.ShapeDtypeStruct((heads, length, 1), jnp.float32),
        ],
        compiler_params=pltpu.CompilerParams(vmem_limit_bytes=40 * 1024 * 1024),
        cost_estimate=pl.CostEstimate(
            flops=4 * heads * length * length * HD,
            bytes_accessed=heads * length * HD * 12,
            transcendentals=heads * length * length,
        ),
        name="attention_forward",
    )(query, key, value, row_ids, col_ids, windows)


def attention_backward(query, key, value, row_ids, col_ids, windows, mixed, logs_in, d_mixed):
    heads, length, _ = query.shape
    blocks, span = windows.shape[1], windows.shape[3]
    rows = length // blocks
    per_block, per_head, rid, cid, window, logs = attention_specs(
        heads, blocks, rows, length, span
    )
    return pl.pallas_call(
        backward_kernel,
        grid=(heads, blocks),
        in_specs=[
            per_block, per_head, per_head, rid, cid, window, per_block, logs, per_block,
        ],
        out_specs=[
            per_block,
            per_head,
            per_head,
            pl.BlockSpec((1, 1, 8, span), lambda h, i: (h, i, 0, 0)),
        ],
        out_shape=[
            jax.ShapeDtypeStruct((heads, length, HD), jnp.bfloat16),
            jax.ShapeDtypeStruct((heads, length, HD), jnp.float32),
            jax.ShapeDtypeStruct((heads, length, HD), jnp.float32),
            jax.ShapeDtypeStruct((heads, blocks, 8, span), jnp.float32),
        ],
        compiler_params=pltpu.CompilerParams(vmem_limit_bytes=40 * 1024 * 1024),
        cost_estimate=pl.CostEstimate(
            flops=10 * heads * length * length * HD,
            bytes_accessed=heads * length * HD * 24,
            transcendentals=heads * length * length,
        ),
        name="attention_backward",
    )(query, key, value, row_ids, col_ids, windows, mixed, logs_in, d_mixed)


def swap_parts(values_in, axis):
    return lax.all_to_all(values_in, axis, split_axis=0, concat_axis=0, tiled=True)


def head_major(rows_in, heads):
    return jnp.transpose(rows_in.reshape(rows_in.shape[0], heads, HD), (1, 0, 2))


def row_major(heads_in):
    heads, length, _ = heads_in.shape
    return jnp.transpose(heads_in, (1, 0, 2)).reshape(length, heads * HD)


def per_device(
    tokens,
    w_query,
    w_key,
    w_value,
    w_output,
    w_router,
    norm_one,
    norm_two,
    rel_bias,
    w_in,
    w_out,
    routes,
    seq_ids,
    buckets,
    d_out,
):
    low = jnp.bfloat16
    members = lax.axis_size("expert")
    shards = lax.axis_size("shard")
    me = lax.axis_index("expert")
    row_count = tokens.shape[1]
    width = tokens.shape[2]
    length = row_count * members
    part_rows = w_query.shape[0]
    table_rows, experts = rel_bias.shape[0], w_router.shape[1]
    heads = -(-H // members)
    lanes = heads * HD
    extra = members * lanes - width

    def own_columns(weight):
        return lax.dynamic_slice_in_dim(
            jnp.pad(weight, ((0, 0), (0, extra))), me * lanes, lanes, 1
        )

    used = 3 * lanes + 2 + experts + H
    packed = jnp.concatenate(
        [
            own_columns(w_query),
            own_columns(w_key),
            own_columns(w_value),
            norm_one[:, None],
            norm_two[:, None],
            w_router,
            jnp.pad(rel_bias, ((0, part_rows - table_rows), (0, 0))),
            jnp.zeros((part_rows, round_up(used, 128) - used), low),
        ],
        axis=1,
    )
    gathered = lax.all_gather(packed, "shard", axis=0, tiled=True)
    rows_all = lax.all_gather(tokens[0], "expert", axis=0, tiled=True)
    output_all = lax.all_gather(w_output, "shard", axis=0, tiled=True)
    weights_qkv = gathered[:, : 3 * lanes]
    at = 3 * lanes
    gain_one_f = gathered[:, at].astype(jnp.float32)
    gain_two_f = gathered[:, at + 1].astype(jnp.float32)
    router_all = gathered[:, at + 2 : at + 2 + experts]
    table_all = gathered[:, at + 2 + experts : used].reshape(shards, part_rows, H)[:, :table_rows]
    table_all = jnp.pad(
        table_all.reshape(shards * table_rows, H), ((0, 0), (0, members * heads - H))
    )
    table_own = lax.dynamic_slice_in_dim(table_all, me * heads, heads, 1)

    flat_rows = tokens[0].astype(jnp.float32)
    h_all, _ = norm_forward(rows_all.astype(jnp.float32), gain_one_f)
    h_all_low = h_all.astype(low)
    qkv = product(h_all_low, weights_qkv).astype(low)
    query = head_major(qkv[:, :lanes] * jnp.asarray(HD**-0.5, low), heads)
    key = head_major(qkv[:, lanes : 2 * lanes], heads)
    value = head_major(qkv[:, 2 * lanes :], heads)
    row_ids = seq_ids[0][:, None]
    col_ids = seq_ids
    bucket_hot = buckets[:, None] == jnp.arange(table_all.shape[0], dtype=jnp.int32)[None, :]
    offset_bias = contract(table_own, bucket_hot.astype(low), 0, 1)
    block = 256 if length % 256 == 0 else length
    blocks = length // block
    span = block + length
    offset_padded = jnp.pad(offset_bias, ((0, 0), (0, 1)))
    windows = jnp.stack(
        [
            offset_padded[:, length - (i + 1) * block : 2 * length - i * block]
            for i in range(blocks)
        ],
        axis=1,
    )[:, :, None, :]
    mixed, log_total = attention_forward(query, key, value, row_ids, col_ids, windows)
    mixed_low = row_major(mixed.astype(low)).reshape(members, row_count, lanes)
    attn_low = jnp.transpose(swap_parts(mixed_low, "expert"), (1, 0, 2)).reshape(
        row_count, members * lanes
    )[:, :width]

    x_one = flat_rows + product(attn_low, output_all)
    h_two, inverse_two = norm_forward(x_one, gain_two_f)
    h_two_low = h_two.astype(low)
    router_probs = jax.nn.softmax(product(h_two_low, router_all), axis=-1)
    route_ids = routes[0, :, 0]
    chosen_int = (route_ids[:, None] == jnp.arange(experts, dtype=jnp.int32)[None, :]).astype(
        jnp.int32
    )
    chosen = chosen_int.astype(jnp.float32)
    gate_value = jnp.sum(router_probs * chosen, axis=1)
    capacity = 2 * row_count // experts
    rank_index = jnp.sum((jnp.cumsum(chosen_int, axis=0) - chosen_int) * chosen_int, axis=1)
    slot_index = route_ids * capacity + rank_index
    slots = experts * capacity
    placement = (
        jnp.arange(slots, dtype=jnp.int32)[:, None] == slot_index[None, :]
    ).astype(low)
    d_two = d_out[0].astype(jnp.float32)
    d_result = (gate_value[:, None] * d_two).astype(low)
    send = product(placement, jnp.concatenate([h_two_low, d_result], axis=1)).astype(low)
    arrived = swap_parts(send.reshape(experts, capacity, 2 * width), "expert").reshape(
        slots, 2 * width
    )
    received, d_received = arrived[:, :width], arrived[:, width:]
    pre_act = product(received, w_in[0])
    act, gelu_back = jax.vjp(lambda u: jax.nn.gelu(u, approximate=True), pre_act)
    act_low = act.astype(low)
    result_rows = product(act_low, w_out[0]).astype(low)
    d_act = contract(d_received, w_out[0], 1, 1)
    d_pre = gelu_back(d_act)[0].astype(low)
    d_entry = contract(d_pre, w_in[0], 1, 1).astype(low)
    back = swap_parts(
        jnp.concatenate([result_rows, d_entry], axis=1).reshape(experts, capacity, 2 * width),
        "expert",
    ).reshape(slots, 2 * width)
    d_w_out_part = contract(act_low, d_received, 0, 0).astype(low)
    d_w_in_part = contract(received, d_pre, 0, 0).astype(low)
    landed = contract(placement, back, 0, 0)
    expert_out, d_h_two = landed[:, :width], landed[:, width:]
    layer_out = (x_one + gate_value[:, None] * expert_out).astype(low)
    d_gate = jnp.sum(d_two * expert_out, axis=1)
    d_logits = router_probs * (chosen * d_gate[:, None] - (gate_value * d_gate)[:, None])
    d_router = jnp.dot(h_two_low.astype(jnp.float32).T, d_logits, precision=HIGHEST)
    d_h_two = d_h_two + jnp.dot(d_logits, router_all.astype(jnp.float32).T, precision=HIGHEST)
    d_x_part, d_gain_two = norm_backward(x_one, inverse_two, gain_two_f, d_h_two)
    d_x_one = d_two + d_x_part
    d_branch = d_x_one.astype(low)
    d_output = contract(attn_low, d_branch, 0, 0).astype(low)
    d_attn = contract(d_branch, output_all, 1, 1).astype(low)

    fold = w_out.shape[1] // width
    d_w_out_folded = jnp.transpose(
        d_w_out_part.reshape(shards, fold, part_rows, width), (0, 2, 1, 3)
    ).reshape(width, fold * width)
    early_used = experts + 1
    early = jnp.concatenate(
        [
            d_w_in_part,
            d_w_out_folded,
            d_output,
            d_router.astype(low),
            d_gain_two.astype(low)[:, None],
            jnp.zeros((width, round_up(early_used, 128) - early_used), low),
        ],
        axis=1,
    )
    early, d_attn = lax.optimization_barrier((early, d_attn))
    early_sum = lax.psum_scatter(early, "shard", scatter_dimension=0, tiled=True)

    d_attn_parts = jnp.transpose(
        jnp.pad(d_attn, ((0, 0), (0, extra))).reshape(row_count, members, lanes), (1, 0, 2)
    )
    d_mixed = head_major(swap_parts(d_attn_parts, "expert").reshape(length, lanes), heads)
    d_query, d_key, d_value, d_windows = attention_backward(
        query, key, value, row_ids, col_ids, windows, mixed, log_total, d_mixed
    )
    d_qkv = jnp.concatenate(
        [row_major(d_query), row_major(d_key.astype(low)), row_major(d_value.astype(low))], axis=1
    )
    d_h_parts = contract(d_qkv, weights_qkv, 1, 1).astype(low)
    d_h_one = jnp.sum(
        swap_parts(d_h_parts.reshape(members, row_count, width), "expert").astype(jnp.float32),
        axis=0,
    )
    d_w_qkv = contract(h_all_low, d_qkv, 0, 0).astype(low)
    d_window = sum(
        jnp.pad(d_windows[:, :, r, : span - (7 - r)], ((0, 0), (0, 0), (7 - r, 0)))
        for r in range(8)
    )
    d_offsets = sum(
        jnp.pad(
            d_window[:, i],
            ((0, 0), (length - (i + 1) * block, i * block)),
        )
        for i in range(blocks)
    )[:, : 2 * length - 1]
    d_table = jnp.einsum(
        "ob,ho->bh", bucket_hot.astype(jnp.float32), d_offsets, precision=HIGHEST
    )
    inverse_one = lax.rsqrt(jnp.mean(flat_rows * flat_rows, axis=-1, keepdims=True) + EPSILON)
    d_x_first, d_gain_one = norm_backward(flat_rows, inverse_one, gain_one_f, d_h_one)
    d_tokens = (d_x_one + d_x_first)[None]

    late_used = 3 * lanes + 1 + heads
    d_table_rows = jnp.pad(
        d_table.astype(low).reshape(shards, table_rows, heads),
        ((0, 0), (0, part_rows - table_rows), (0, 0)),
    ).reshape(width, heads)
    late = jnp.concatenate(
        [
            d_w_qkv,
            d_gain_one.astype(low)[:, None],
            d_table_rows,
            jnp.zeros((width, round_up(late_used, 128) - late_used), low),
        ],
        axis=1,
    )
    late_sum = jnp.sum(
        swap_parts(late.reshape(shards, part_rows, late.shape[1]), "shard").astype(jnp.float32),
        axis=0,
    ).astype(low)
    both = jnp.concatenate([late_sum, early_sum[:, 2 * w_in.shape[2] :]], axis=1)
    all_parts = lax.all_gather(both, "expert", axis=0, tiled=False).astype(jnp.float32)

    def joined(start, size):
        taken = all_parts[:, :, start : start + size]
        return jnp.transpose(taken, (1, 0, 2)).reshape(part_rows, members * size)

    late_width = late.shape[1]
    total_q = joined(0, lanes)[:, :width]
    total_k = joined(lanes, lanes)[:, :width]
    total_v = joined(2 * lanes, lanes)[:, :width]
    total_one = jnp.sum(all_parts[:, :, 3 * lanes], axis=0)
    total_table = joined(3 * lanes + 1, heads)[:table_rows, :H]
    summed = jnp.sum(all_parts[:, :, late_width:], axis=0)
    total_o = summed[:, :width]
    total_router = summed[:, width : width + experts]
    total_two = summed[:, width + experts]
    ff = w_in.shape[2]
    grad_in = early_sum[:, :ff].astype(jnp.float32)[None]
    grad_out = jnp.transpose(
        early_sum[:, ff : 2 * ff].reshape(part_rows, fold, width), (1, 0, 2)
    ).reshape(1, fold * part_rows, width).astype(jnp.float32)
    return (
        layer_out[None],
        d_tokens,
        total_q,
        total_k,
        total_v,
        total_o,
        total_router,
        total_one,
        total_two,
        total_table,
        grad_in,
        grad_out,
    )


def solution(mesh):
    placed = (
        P("shard", "expert", None),
        P("shard", None),
        P("shard", None),
        P("shard", None),
        P("shard", None),
        P("shard", None),
        P("shard"),
        P("shard"),
        P("shard", None),
        P("expert", None, None),
        P("expert", None, None),
        P("shard", "expert", None),
        P("shard", None),
        P(),
        P("shard", "expert", None),
    )
    return jax.shard_map(
        per_device,
        mesh=mesh,
        in_specs=placed,
        out_specs=(
            P("shard", "expert", None),
            P("shard", "expert", None),
            P("shard", None),
            P("shard", None),
            P("shard", None),
            P("shard", None),
            P("shard", None),
            P("shard"),
            P("shard"),
            P("shard", None),
            P("expert", "shard", None),
            P("expert", "shard", None),
        ),
        check_vma=False,
    )
```

time: 1080 us -> 436 us (0.40)
  waiting for transfers between devices: 515 us -> 126 us
  local copies, waits for them, and re-layouts: 251 us -> 71.1 us
  matrix products: 127 us -> 51.3 us
  Pallas kernels: 0 us -> 28.6 us
  other arithmetic: 38 us -> 20.5 us
    reduce_scatter x7 -> x1, waiting for transfers between devices: 404 us -> 80.5 us  [per_device(): lax.psum_scatter(early, 'shard', scatter_dimension=0, tiled=True)]
    dot_general x30 -> x11, matrix products: 102 us -> 33 us  [the longest x10 32.4 us: contract(): lax.dot_general(left, right, (((left_dim,), (right_dim,)), ((), ())), pre...]
    all_to_all x0 -> x2, blocking collectives: none -> 63.9 us  [swap_parts(): lax.all_to_all(values_in, axis, split_axis=0, concat_axis=0, tiled=True)]
    unnamed x2 -> x0, blocking collectives: 60.4 us -> none
    unnamed x117 -> x94, local copies, waits for them, and re-layouts: 65.6 us -> 17.4 us
    reshape x3 -> x8, local copies, waits for them, and re-layouts: 57.7 us -> 9.84 us  [the longest x1 3.65 us: per_device(): d_w_out_part.reshape(shards, fold, part_rows, width)]
    all_gather x6 -> x3, waiting for transfers between devices: 55.3 us -> 12.6 us  [the longest x1 12.5 us: per_device(): lax.all_gather(both, 'expert', axis=0, tiled=False).astype(jnp.float32)]
    slice x5 -> x14, local copies, waits for them, and re-layouts: 41.4 us -> 4.53 us  [the longest x1 1.04 us: per_device(): both = jnp.concatenate([late_sum, early_sum[:, 2 * w_in.shape[2]:]], axis=1)]
  transfers between devices with their start and end apart: 19 -> 8, of which waited for: 12 -> 6; matrix products, arithmetic and copies ran while one was open for 31% -> 15% of each run, Pallas kernels for 0% -> 7%
where the time goes in v1:
time: 436 us; the launch traced here: 428 us
  waiting for transfers between devices  126 us (29%)
  blocking collectives  99.6 us (23%)
  local copies, waits for them, and re-layouts  71.1 us (16%)
  matrix products  51.3 us (12%)
  Pallas kernels  28.6 us (7%)
  other arithmetic  20.5 us (5%)
  starting transfers between devices  16.2 us (4%)
  between operations  15 us (3%)
    reduce_scatter x1, waiting for transfers between devices, per_device(): lax.psum_scatter(early, 'shard', scatter_dimension=0, tiled=True)  80.5 us
    all_to_all x2, blocking collectives, swap_parts(): lax.all_to_all(values_in, axis, split_axis=0, concat_axis=0, tiled=True)  63.9 us
    all_gather x1, blocking collectives, per_device(): gathered = lax.all_gather(packed, 'shard', axis=0, tiled=True)  35.7 us
    dot_general x10, matrix products, contract(): lax.dot_general(left, right, (((left_dim,), (right_dim,)), ((), ())), pre...  32.4 us
    all_to_all x4, waiting for transfers between devices, swap_parts(): lax.all_to_all(values_in, axis, split_axis=0, concat_axis=0, tiled=True)  31.7 us
    unnamed x94, local copies, waits for them, and re-layouts  17.4 us
    concatenate x1, local copies, waits for them, and re-layouts, per_device(): jnp.concatenate([d_w_in_part, d_w_out_folded, d_output, d_router.astype(l...  17.2 us
    all_to_all x4, starting transfers between devices, swap_parts(): lax.all_to_all(values_in, axis, split_axis=0, concat_axis=0, tiled=True)  15.9 us
  transfers between devices with their start and end apart: 8, of which 6 were waited for; matrix products, arithmetic and copies ran while one was open for 15% of the time, Pallas kernels for 7%

profile of v1, /device:TPU:0, one launch (start us, length us, event | category | flops | bytes accessed | tf_op | source)
XLA Modules:
  0.0 428.3 jit_solution(1436249287915980678)
XLA Ops:
  9.4 1.2 reduce-window.6
  13.3 1.7 copy.220.row_ids_ref
  17.0 35.7 %all_gather.16 = bf16[768,640]{1,0:T(8,128)(2,1)S(1)} all-gather(bf16[96,640]{1,0:T(8,128)(2,1)S(1)} %concatenate.24), channel_id=1, replica_groups=mesh['expert'=4,'shard'=8] {'shard'}, dimensions={0}, use_global_device_ids=true | all-gather | bytes 1105920 | tf_op jit(solution)/shard_map/all_gather | solution.py:241
  53.9 1.8 fusion.15
  55.7 2.7 convolution_convert_fusion.5
  59.7 1.7 copy.219
  64.7 13.2 %attention_forward.1 = (f32[3,1024,64]{2,1,0:T(8,128)S(1)}, f32[3,1024,1]{2,1,0:T(8,128)S(1)}) custom-call(bf16[3,1024,64]{2,1,0:T(8,128)(2,1)S(1)} %bitcast.154, bf16[3,1024,64]{2,1,0:T(8,128)(2,1)S(1)} %bitcast.150, bf16[3,1024,64]{2,1,0:T(8,128)(2,1)S(1)} %bitcast.152, s32[1024,1]{1,0:T(8,128)S(1)} %copy-done.12, s32[1,1024]{1,0:T(1,128)S(1)} %copy-done.14, ...), custom_call_target="tpu_custom_call" | custom-call | flops 805306368 | bytes 2359296 | tf_op jit(solution)/shard_map/attention_forward/pallas_call | solution.py:125
  80.6 3.5 all-to-all-start
  84.1 7.3 %all-to-all-done = bf16[4,256,192]{1,2,0:T(8,128)(2,1)S(1)} async-done(((bf16[4,256,192]{1,2,0:T(8,128)(2,1)}), bf16[4,256,192]{1,2,0:T(8,128)(2,1)S(1)}, u32[]{:S(2)}, u32[]{:S(2)}) %all-to-all-start) | async-done | bytes 393248 | tf_op jit(solution)/shard_map/all_to_all | solution.py:180
  91.4 2.0 multiply_reduce_fusion.2
  93.6 1.3 fusion.92
  96.7 23.3 %all_to_all.30 = bf16[4,128,1536]{2,1,0:T(8,128)(2,1)S(1)} all-to-all(bf16[4,128,1536]{2,1,0:T(8,128)(2,1)S(1)} %bitcast.162), channel_id=1, replica_groups=mesh['expert'=4,'shard'=8] {'expert'}, dimensions={0} | all-to-all | bytes 3145728 | tf_op jit(solution)/shard_map/all_to_all | solution.py:180
  120.0 5.1 %fusion.13 = f32[512,3072]{1,0:T(8,128)S(1)} fusion(bf16[1,768,3072]{2,1,0:T(8,128)(2,1)} %param.24, bf16[512,1536]{1,0:T(8,128)(2,1)S(1)} %bitcast.171), kind=kOutput, calls=%fused_computation.18 | convolution fusion | flops 2415919104 | bytes 11796480 | tf_op jit(solution)/shard_map/dot_general | solution.py:17
  125.1 3.8 fusion.25
  128.9 6.1 %fusion.6 = bf16[512,3072]{1,0:T(8,128)(2,1)S(1)} fusion(f32[512,3072]{1,0:T(8,128)S(1)} %fusion.13, bf16[1,3072,768]{2,1,0:T(8,128)(2,1)S(1)} %bitcast.203, bf16[512,1536]{1,0:T(8,128)(2,1)S(1)} %bitcast.172), kind=kOutput, calls=%fused_computation.8 | convolution fusion | flops 2447376384 | bytes 14942208 | tf_op jit(solution)/shard_map/dot_general | solution.py:21
  135.1 2.7 fusion.22
  137.8 1.3 pad_maximum_fusion
  139.1 4.3 %all-to-all-start.2 = ((bf16[4,128,1536]{2,1,0:T(8,128)(2,1)}), bf16[4,128,1536]{2,1,0:T(8,128)(2,1)}, u32[]{:S(2)}, u32[]{:S(2)}) async-start(bf16[4,128,1536]{2,1,0:T(8,128)(2,1)} %bitcast.161), calls=%async_computation.2 | async-start | bytes 3145728 | tf_op jit(solution)/shard_map/all_to_all | solution.py:180
  143.6 6.3 %convolution_convert_fusion = bf16[3072,768]{1,0:T(8,128)(2,1)S(1)} fusion(bf16[512,1536]{1,0:T(8,128)(2,1)} %bitcast.173, f32[512,3072]{1,0:T(8,128)} %copy-done.36), kind=kOutput, calls=%fused_computation.10 | convolution fusion | flops 2432434176 | bytes 11796480 | tf_op jit(solution)/shard_map/dot_general | solution.py:21
  149.9 3.6 copy.225
  153.6 3.2 copy.264
  156.8 4.5 %convolution_convert_fusion.1 = bf16[768,3072]{1,0:T(8,128)(2,1)} fusion(bf16[512,3072]{1,0:T(8,128)(2,1)S(1)} %copy-done.38, bf16[512,1536]{1,0:T(8,128)(2,1)S(1)} %bitcast.174), kind=kOutput, calls=%fused_computation.11 | convolution fusion | flops 2418278400 | bytes 8650752 | tf_op jit(solution)/shard_map/dot_general | solution.py:21
  161.4 2.2 all-to-all-done.2
  163.6 2.0 fusion.51
  166.5 2.6 multiply_reduce_fusion
  170.4 1.5 convert_add_fusion.1
  171.9 2.8 convolution_convert_fusion.4
  174.7 17.2 %concatenate.27 = bf16[768,7040]{1,0:T(8,128)(2,1)} concatenate(bf16[768,3072]{1,0:T(8,128)(2,1)} %convolution_convert_fusion.1, bf16[768,3072]{1,0:T(8,128)(2,1)} %bitcast.160, bf16[768,768]{1,0:T(8,128)(2,1)} %convolution_convert_fusion.4, bf16[768,4]{1,0:T(8,128)(2,1)S(1)} %copy.227, bf16[768,1]{1,0:T(8,128)(2,1)} %convert_element_type.249, bf16[768,123]{1,0:T(8,128)(2,1)S(1)} %broadcast_in_dim.26), dimensions={1} | concatenate | bytes 21626880 | tf_op jit(solution)/shard_map/concatenate | solution.py:338
  191.9 1.8 convolution_convert_fusion.7
  194.7 3.5 all-to-all-start.3
  198.3 7.2 %all-to-all-done.3 = bf16[4,256,192]{1,2,0:T(8,128)(2,1)S(1)} async-done(((bf16[4,256,192]{1,2,0:T(8,128)(2,1)}), bf16[4,256,192]{1,2,0:T(8,128)(2,1)S(1)}, u32[]{:S(2)}, u32[]{:S(2)}) %all-to-all-start.3) | async-done | bytes 393248 | tf_op jit(solution)/shard_map/all_to_all | solution.py:180
  212.9 1.4 copy-done.16
  214.3 15.3 %attention_backward.1 = (bf16[3,1024,64]{2,1,0:T(8,128)(2,1)S(1)}, f32[3,1024,64]{2,1,0:T(8,128)S(1)}, f32[3,1024,64]{2,1,0:T(8,128)S(1)}, f32[3,4,8,1280]{3,2,1,0:T(8,128)S(1)}) custom-call(bf16[3,1024,64]{2,1,0:T(8,128)(2,1)S(1)} %bitcast.155, bf16[3,1024,64]{2,1,0:T(8,128)(2,1)S(1)} %bitcast.151, bf16[3,1024,64]{2,1,0:T(8,128)(2,1)S(1)} %bitcast.153, ...), custom_call_target="tpu_custom_call" | custom-call | flops 2013265920 | bytes 4718592 | tf_op jit(solution)/shard_map/attention_backward/pallas_call | solution.py:151
  232.7 2.1 copy.233
  235.9 2.3 copy.234
  239.1 1.4 copy.235
  240.5 3.6 convolution_convert_fusion.3
  244.2 4.6 %all-to-all-start.4 = ((bf16[4,256,768]{2,1,0:T(8,128)(2,1)}), bf16[4,256,768]{2,1,0:T(8,128)(2,1)}, u32[]{:S(2)}, u32[]{:S(2)}) async-start(bf16[4,256,768]{2,1,0:T(8,128)(2,1)} %bitcast.170), calls=%async_computation.4 | async-start | bytes 3145728 | tf_op jit(solution)/shard_map/all_to_all | solution.py:180
  250.1 2.1 convolution_convert_fusion.6
  252.2 1.8 copy.236
  254.0 14.9 %all-to-all-done.4 = bf16[4,256,768]{2,1,0:T(8,128)(2,1)} async-done(((bf16[4,256,768]{2,1,0:T(8,128)(2,1)}), bf16[4,256,768]{2,1,0:T(8,128)(2,1)}, u32[]{:S(2)}, u32[]{:S(2)}) %all-to-all-start.4) | async-done | bytes 1572896 | tf_op jit(solution)/shard_map/all_to_all | solution.py:180
  268.9 1.7 convert_reduce_fusion
  271.6 40.6 %all_to_all.31 = bf16[8,96,640]{2,1,0:T(8,128)(2,1)S(1)} all-to-all(bf16[8,96,640]{2,1,0:T(8,128)(2,1)S(1)} %fusion.30), channel_id=1, replica_groups=mesh['expert'=4,'shard'=8] {'shard'}, dimensions={0} | all-to-all | bytes 1966080 | tf_op jit(solution)/shard_map/all_to_all | solution.py:180
  312.3 80.5 %reduce-scatter.2.cloned.1.call-done = bf16[96,7040]{1,0:T(8,128)(2,1)} async-done(((bf16[768,7040]{1,0:T(8,128)(2,1)}), bf16[96,7040]{1,0:T(8,128)(2,1)}) %reduce-scatter.2.cloned.1.call-update) | async-done | bytes 1351696 | tf_op jit(solution)/shard_map/reduce_scatter | solution.py:350
  395.8 1.3 slice_convert_fusion
  397.6 1.2 copy.253
  398.9 12.5 %all-gather.10.cloned.1.call-done = bf16[384,1536]{1,0:T(8,128)(2,1)} async-done(((bf16[96,1536]{1,0:T(8,128)(2,1)}), bf16[384,1536]{1,0:T(8,128)(2,1)}) %all-gather.10.cloned.1.call-update) | async-done | bytes 1179664 | tf_op jit(solution)/shard_map/all_gather | solution.py:405
  412.4 1.5 convert.11
  (199 shorter events, 47.4 us)
Async XLA Ops:
  7.2 8.5 %copy-start = (bf16[96,768]{1,0:T(8,128)(2,1)S(1)}, bf16[96,768]{1,0:T(8,128)(2,1)}, u32[]{:S(2)}) copy-start(bf16[96,768]{1,0:T(8,128)(2,1)} %param.16) | copy-start | bytes 442372
  7.2 45.6 %copy-start.35 = (s32[2047]{0:T(1024)S(1)}, s32[2047]{0:T(1024)}, u32[]{:S(2)}) copy-start(s32[2047]{0:T(1024)} %param.28) | copy-start | bytes 24568
  7.2 46.7 %all-gather.8.cloned.1.call-start = ((), (), s32[]{:S(2)}) async-start(), calls=%async_computation.9 | async-start | bytes 1966080 | tf_op jit(solution)/shard_map/all_gather | solution.py:242
  7.9 76.2 %all-gather.6.cloned.1.call-start = ((), (), s32[]{:S(2)}) async-start(), calls=%async_computation.7 | async-start | bytes 1327104 | tf_op jit(solution)/shard_map/all_gather | solution.py:243
  52.6 5.8 %copy-start.22 = (bf16[768,640]{1,0:T(8,128)(2,1)}, bf16[768,640]{1,0:T(8,128)(2,1)S(1)}, u32[]{:S(2)}) copy-start(bf16[768,640]{1,0:T(8,128)(2,1)S(1)} %all_gather.16) | copy-start | bytes 2949124
  58.5 4.1 copy-start.14
  59.7 18.3 %copy-start.4 = (bf16[1024,3,64]{2,0,1:T(8,128)(2,1)}, bf16[1024,3,64]{2,0,1:T(8,128)(2,1)S(1)}, u32[]{:S(2)}) copy-start(bf16[1024,3,64]{2,0,1:T(8,128)(2,1)S(1)} %copy.218) | copy-start | bytes 1179652
  61.4 16.6 %copy-start.6 = (bf16[1024,3,64]{2,0,1:T(8,128)(2,1)}, bf16[1024,3,64]{2,0,1:T(8,128)(2,1)S(1)}, u32[]{:S(2)}) copy-start(bf16[1024,3,64]{2,0,1:T(8,128)(2,1)S(1)} %copy.219) | copy-start | bytes 1179652
  62.5 1.1 copy-start.8
  78.0 1.2 copy-start.15
  79.1 4.9 %copy-start.34 = (s32[1,256,1]{1,2,0:T(1,128)S(1)}, s32[1,256,1]{1,2,0:T(1,128)}, u32[]{:S(2)}) copy-start(s32[1,256,1]{1,2,0:T(1,128)} %param.26) | copy-start | bytes 3076
  79.1 12.3 %copy-start.19 = (bf16[1,256,768]{2,1,0:T(8,128)(2,1)S(1)}, bf16[1,256,768]{2,1,0:T(8,128)(2,1)}, u32[]{:S(2)}) copy-start(bf16[1,256,768]{2,1,0:T(8,128)(2,1)} %param.15) | copy-start | bytes 1179652
  80.6 10.9 %all-to-all-start = ((bf16[4,256,192]{1,2,0:T(8,128)(2,1)}), bf16[4,256,192]{1,2,0:T(8,128)(2,1)S(1)}, u32[]{:S(2)}, u32[]{:S(2)}) async-start(bf16[4,256,192]{1,2,0:T(8,128)(2,1)} %copy.222), calls=%async_computation | async-start | bytes 786432 | tf_op jit(solution)/shard_map/all_to_all | solution.py:180
  91.4 5.3 %copy-start.24 = (bf16[4,256,192]{1,2,0:T(8,128)(2,1)}, bf16[4,256,192]{1,2,0:T(8,128)(2,1)S(1)}, u32[]{:S(2)}) copy-start(bf16[4,256,192]{1,2,0:T(8,128)(2,1)S(1)} %all-to-all-done) | copy-start | bytes 1179652
  96.7 28.4 %slice-start = ((s8[4718592]{0:T(1024)(128)(4,1)}), s8[4194304]{0:T(1024)(128)(4,1)S(1)}, s32[]{:S(2)}) async-start(s8[4718592]{0:T(1024)(128)(4,1)} %bitcast.202), calls=%async_computation.11 | async-start | bytes 8388608
  120.0 8.9 %copy-start.28 = (bf16[4,128,1536]{2,1,0:T(8,128)(2,1)}, bf16[4,128,1536]{2,1,0:T(8,128)(2,1)S(1)}, u32[]{:S(2)}) copy-start(bf16[4,128,1536]{2,1,0:T(8,128)(2,1)S(1)} %all_to_all.30) | copy-start | bytes 4718596
  120.0 5.1 %slice-start.1 = ((s8[4718592]{0:T(1024)(128)(4,1)}), s8[524288]{0:T(1024)(128)(4,1)S(1)}, s32[]{:S(2)}) async-start(s8[4718592]{0:T(1024)(128)(4,1)} %bitcast.202), calls=%async_computation.12 | async-start | bytes 1048576
  125.1 3.8 copy-start.36
  125.1 9.9 %slice-start.2 = ((s8[4718592]{0:T(1024)(128)(4,1)}), s8[4194304]{0:T(1024)(128)(4,1)S(1)}, s32[]{:S(2)}) async-start(s8[4718592]{0:T(1024)(128)(4,1)} %bitcast.204), calls=%async_computation.13 | async-start | bytes 8388608
  128.9 6.1 %slice-start.3 = ((s8[4718592]{0:T(1024)(128)(4,1)}), s8[524288]{0:T(1024)(128)(4,1)S(1)}, s32[]{:S(2)}) async-start(s8[4718592]{0:T(1024)(128)(4,1)} %bitcast.204), calls=%async_computation.14 | async-start | bytes 1048576
  135.1 2.7 copy-start.37
  139.1 24.5 %all-to-all-start.2 = ((bf16[4,128,1536]{2,1,0:T(8,128)(2,1)}), bf16[4,128,1536]{2,1,0:T(8,128)(2,1)}, u32[]{:S(2)}, u32[]{:S(2)}) async-start(bf16[4,128,1536]{2,1,0:T(8,128)(2,1)} %bitcast.161), calls=%async_computation.2 | async-start | bytes 3145728 | tf_op jit(solution)/shard_map/all_to_all | solution.py:180
  143.4 249.4 %reduce-scatter.2.cloned.1.call-start = ((), (), s32[]{:S(2)}) async-start(), calls=%async_computation.8 | async-start | bytes 12165120 | tf_op jit(solution)/shard_map/reduce_scatter | solution.py:350
  153.5 3.3 copy-start.29
  153.6 3.3 copy-start.38
  161.3 4.2 copy-start.25
  171.9 20.0 %copy-start.17 = (f32[256,768]{1,0:T(8,128)}, f32[256,768]{1,0:T(8,128)S(1)}, u32[]{:S(2)}) copy-start(f32[256,768]{1,0:T(8,128)S(1)} %convert_add_fusion.1) | copy-start | bytes 2359300
  193.7 4.5 %copy-start.20 = (bf16[1,256,768]{2,1,0:T(8,128)(2,1)S(1)}, bf16[1,256,768]{2,1,0:T(8,128)(2,1)}, u32[]{:S(2)}) copy-start(bf16[1,256,768]{2,1,0:T(8,128)(2,1)} %param.15) | copy-start | bytes 1179652
  194.7 10.9 %all-to-all-start.3 = ((bf16[4,256,192]{1,2,0:T(8,128)(2,1)}), bf16[4,256,192]{1,2,0:T(8,128)(2,1)S(1)}, u32[]{:S(2)}, u32[]{:S(2)}) async-start(bf16[4,256,192]{1,2,0:T(8,128)(2,1)} %bitcast.35), calls=%async_computation.3 | async-start | bytes 786432 | tf_op jit(solution)/shard_map/all_to_all | solution.py:180
  207.3 1.1 copy-start.5
  208.4 1.1 copy-start.7
  209.6 1.1 copy-start.9
  210.7 1.1 copy-start.11
  212.9 1.4 copy-start.16
  229.7 1.2 copy-start.2
  231.7 3.2 copy-start.3
  235.9 4.6 %copy-start.23 = (bf16[768,640]{1,0:T(8,128)(2,1)S(1)}, bf16[768,640]{1,0:T(8,128)(2,1)}, u32[]{:S(2)}) copy-start(bf16[768,640]{1,0:T(8,128)(2,1)} %copy-done.22) | copy-start | bytes 2949124
  235.9 4.6 %copy-start.31 = (bf16[1024,3,64]{0,2,1:T(8,128)(2,1)S(1)}, bf16[1024,3,64]{0,2,1:T(8,128)(2,1)}, u32[]{:S(2)}) copy-start(bf16[1024,3,64]{0,2,1:T(8,128)(2,1)} %copy.233) | copy-start | bytes 1179652
  244.2 4.7 %copy-start.26 = (f32[3,4,8,1280]{3,1,0,2:T(4,128)S(1)}, f32[3,4,8,1280]{3,1,0,2:T(4,128)}, u32[]{:S(2)}) copy-start(f32[3,4,8,1280]{3,1,0,2:T(4,128)} %copy.237) | copy-start | bytes 1474564
  244.2 5.9 %copy-start.27 = (bf16[1,1024,768]{2,1,0:T(8,128)(2,1)S(1)}, bf16[1,1024,768]{2,1,0:T(8,128)(2,1)}, u32[]{:S(2)}) copy-start(bf16[1,1024,768]{2,1,0:T(8,128)(2,1)} %all-gather.8.cloned.1.call-done) | copy-start | bytes 4718596
  244.2 5.9 %copy-start.32 = (bf16[1024,3,64]{0,2,1:T(8,128)(2,1)S(1)}, bf16[1024,3,64]{0,2,1:T(8,128)(2,1)}, u32[]{:S(2)}) copy-start(bf16[1024,3,64]{0,2,1:T(8,128)(2,1)} %copy.233) | copy-start | bytes 1179652
  244.2 5.9 %copy-start.33 = (bf16[1024,3,64]{0,2,1:T(8,128)(2,1)S(1)}, bf16[1024,3,64]{0,2,1:T(8,128)(2,1)}, u32[]{:S(2)}) copy-start(bf16[1024,3,64]{0,2,1:T(8,128)(2,1)} %copy.234) | copy-start | bytes 1179652
  244.2 24.8 %all-to-all-start.4 = ((bf16[4,256,768]{2,1,0:T(8,128)(2,1)}), bf16[4,256,768]{2,1,0:T(8,128)(2,1)}, u32[]{:S(2)}, u32[]{:S(2)}) async-start(bf16[4,256,768]{2,1,0:T(8,128)(2,1)} %bitcast.170), calls=%async_computation.4 | async-start | bytes 3145728 | tf_op jit(solution)/shard_map/all_to_all | solution.py:180
  248.8 162.6 %all-gather.10.cloned.1.call-start = ((), (), s32[]{:S(2)}) async-start(), calls=%async_computation.10 | async-start | bytes 1474560 | tf_op jit(solution)/shard_map/all_gather | solution.py:405
  252.2 18.4 %copy-start.21 = (bf16[1,256,768]{2,1,0:T(8,128)(2,1)S(1)}, bf16[1,256,768]{2,1,0:T(8,128)(2,1)}, u32[]{:S(2)}) copy-start(bf16[1,256,768]{2,1,0:T(8,128)(2,1)} %param.15) | copy-start | bytes 1179652
  271.3 123.4 %copy-start.18 = (f32[256,768]{1,0:T(8,128)S(1)}, f32[256,768]{1,0:T(8,128)}, u32[]{:S(2)}) copy-start(f32[256,768]{1,0:T(8,128)} %copy-done.17) | copy-start | bytes 2359300
  392.8 3.0 copy-start.30
  414.8 6.8 %copy-start.1 = (bf16[96,768]{1,0:T(8,128)(2,1)S(1)}, bf16[96,768]{1,0:T(8,128)(2,1)}, u32[]{:S(2)}) copy-start(bf16[96,768]{1,0:T(8,128)(2,1)} %param.16) | copy-start | bytes 442372
  (3 other events, 3.0 us)
Sparse Core Ops, SparseCore 0:
  9.6 22.3 all-gather.7
  34.2 42.4 all-gather.5
  193.8 198.9 reduce-scatter.1
  394.8 16.5 all-gather.9
